TPU v7x, 128 devices: a whole 4x4x4 slice. The times are simulated.
128 devices in a mesh: layer: 2 (over core), feat: 32 (over z_lo, y, x), dp: 2 (over z_hi).
Axes of the slice: x: 4, y: 4, z: 4 (z_hi: 2, z_lo: 2; z = z_hi * 2 + z_lo), core: 2. Of those that a mesh axis runs over, the one named last changes fastest.
Arguments:
- acts: bfloat16 [2, 2048, 3584], P('layer', 'dp', 'feat'), may hold values from -6 to 6
- targets: bfloat16 [2, 2048, 3584], P('layer', 'dp', 'feat'), may hold values from -6 to 6
- enc: bfloat16 [2, 3584, 16384], P('layer', None, 'feat'), may hold values from -0.09375 to 0.09375
- enc_bias: float32 [2, 16384], P('layer', 'feat'), may hold values from -1 to 0.5
- dec_own: bfloat16 [2, 16384, 3584], P('layer', 'feat'), may hold values from -0.046875 to 0.046875
- dec_cross: bfloat16 [16384, 3584], P('feat', 'layer'), may hold values from -0.046875 to 0.046875
- dec_bias: bfloat16 [2, 3584], P('layer', 'feat'), may hold values from -3 to 3
Outputs:
- residual: float32 [2, 2048, 3584], P('layer', 'dp', 'feat')
- grad_enc: float32 [2, 3584, 16384], P('layer', 'dp', 'feat')
- grad_dec_own: float32 [2, 16384, 3584], P('layer', 'feat', 'dp')
- grad_dec_cross: float32 [16384, 3584], P('feat', ('layer', 'dp'))
All inputs are finite; a program needn't handle non-finite values.
Results may differ from a plain program's by a relative error of at most 0.025.
Values may be sent and summed in bfloat16 or wider, within the bound.
A program may use at most 192 MiB of HBM per device.

v0:
```python
import functools

import jax
import jax.numpy as jnp
from jax import lax
from jax.experimental import pallas as pl
from jax.experimental.pallas import tpu as pltpu
from jax.sharding import PartitionSpec as P

MESH = pl.DeviceIdType.MESH
ALL = slice(None)
SIDE = 4
JOBS = 8


class Place:
    def __init__(self):
        feat = lax.axis_index("feat")
        self.core = lax.axis_index("layer")
        self.dp = lax.axis_index("dp")
        self.x = lax.rem(feat, SIDE)
        self.y = lax.rem(lax.div(feat, SIDE), SIDE)
        self.zl = lax.div(feat, SIDE * SIDE)

    def feat(self, zl=None, y=None, x=None):
        zl = self.zl if zl is None else zl
        y = self.y if y is None else y
        x = self.x if x is None else x
        return (zl * SIDE + y) * SIDE + x

    def at(self, axis):
        return self.x if axis == "x" else self.y

    def along(self, axis, step):
        return lax.rem(self.at(axis) + (step + SIDE), SIDE)

    def neighbour(self, axis, step):
        return {"feat": self.feat(**{axis: self.along(axis, step)})}

    def pair(self):
        return {"feat": self.feat(zl=1 - self.zl)}

    def across(self, zl):
        return {"feat": self.feat(zl=zl), "dp": 1 - self.dp}

    def other_core(self):
        return {"layer": 1 - self.core}

    def greet(self):
        peers = [self.neighbour(a, s) for a in "xy" for s in (1, -1)]
        peers += [self.pair(), self.across(0), self.across(1)]
        peers.append(self.other_core())
        peers += [dict(self.pair(), **self.other_core()), dict(self.across(1 - self.zl), **self.other_core())]
        barrier = pltpu.get_barrier_semaphore()
        for peer in peers:
            pl.semaphore_signal(barrier, inc=1, device_id=peer, device_id_type=MESH)
        pl.semaphore_wait(barrier, len(peers))


def remote(src, dst, send, recv, device):
    return pltpu.make_async_remote_copy(
        src_ref=src, dst_ref=dst, send_sem=send, recv_sem=recv, device_id=device, device_id_type=MESH
    )


class Gather:
    sems = 11
    steps = 6

    whole, right, left = (slice(0, 2), ALL), (slice(0, 1), ALL), (slice(1, 2), ALL)

    def __init__(self, place, buf, own, lanes, flip, send, recv, local, job):
        self.place, self.buf, self.own, self.lanes = place, buf, own, lanes
        self.first, self.second = ("y", "x") if flip else ("x", "y")
        self.send, self.recv, self.local, self.job = send, recv, local, job
        self.sent = []

    def first_block(self, part, at):
        p = self.place
        slots, rows = part
        index = (slots, p.y, at, rows, self.lanes) if self.first == "x" else (slots, at, p.x, rows, self.lanes)
        return self.buf.at[index]

    def second_block(self, part, at):
        slots, rows = part
        index = (slots, at, ALL, rows, self.lanes) if self.second == "y" else (slots, ALL, at, rows, self.lanes)
        return self.buf.at[index]

    def copy(self, sem, src, dst, device, recv=None):
        return remote(src, dst, self.send.at[self.job, sem], self.recv.at[self.job, sem if recv is None else recv], device)

    def out(self, sem, block, device):
        copy = self.copy(sem, block, block, device)
        copy.start()
        self.sent.append(copy)
        return copy

    def ring(self, sem, axis, block):
        p = self.place
        own = block(self.whole, p.at(axis))
        return (self.out(sem, own, p.neighbour(axis, 1)), self.out(sem + 1, own, p.neighbour(axis, -1)))

    def forward(self, sem, axis, block):
        p = self.place
        return (
            self.out(sem, block(self.right, p.along(axis, -1)), p.neighbour(axis, 1)),
            self.out(sem + 1, block(self.left, p.along(axis, 1)), p.neighbour(axis, -1)),
        )

    def begin(self):
        p = self.place
        here = self.buf.at[p.zl, p.y, p.x, :, self.lanes]
        self.kept = pltpu.make_async_copy(self.own, here, self.local.at[self.job])
        self.kept.start()
        self.waits = [self.copy(0, self.own, here, p.pair())]
        self.waits[0].start()
        self.sent += self.waits

    def settle(self):
        self.kept.wait()

    def step(self, number):
        if number == 0:
            self.begin()
            return
        for copy in self.waits:
            copy.wait_recv()
        if number == 1:
            self.settle()
            self.waits = self.ring(3, self.first, self.first_block)
        elif number == 2:
            self.waits = self.forward(5, self.first, self.first_block)
        elif number == 3:
            self.waits = self.ring(7, self.second, self.second_block)
        elif number == 4:
            self.waits = self.forward(9, self.second, self.second_block)

    def finish(self):
        for copy in self.sent:
            copy.wait_send()


class Extra(Gather):
    def __init__(self, *args):
        super().__init__(*args)
        rows = self.own.shape[0]
        cut = (rows // 32 + rows % 32 // 16) * 16
        slot = slice(2, 3)
        self.whole, self.right, self.left = (slot, ALL), (slot, pl.ds(0, cut)), (slot, pl.ds(cut, rows - cut))

    def begin(self):
        p = self.place
        there = self.buf.at[2, p.y, p.x, :, self.lanes]
        self.cross = [self.copy(1 + zl, self.own, there, p.across(zl), recv=1) for zl in (0, 1)]

        @pl.when(p.zl != p.dp)
        def _():
            for copy in self.cross:
                copy.start()

        self.waits = [self.cross[0]]

    def settle(self):
        pass

    def finish(self):
        super().finish()

        @pl.when(self.place.zl != self.place.dp)
        def _():
            for copy in self.cross:
                copy.wait_send()


class Reduce:
    sems = 13
    steps = 6

    def __init__(self, place, part, lanes, flip, room, send, recv, job, finish):
        self.place, self.part, self.lanes = place, part, lanes
        self.first, self.second = ("x", "y") if flip else ("y", "x")
        self.far1, self.far2, self.near1, self.near2, self.last = room
        self.send, self.recv, self.job, self.done = send, recv, job, finish
        self.sent = []

    def first_block(self, z, at):
        return (z, at, ALL, ALL, self.lanes) if self.first == "y" else (z, ALL, at, ALL, self.lanes)

    def second_block(self, z, at):
        p = self.place
        return (z, p.y, at, ALL, self.lanes) if self.first == "y" else (z, at, p.x, ALL, self.lanes)

    def out(self, sem, src, dst, device):
        copy = remote(src, dst, self.send.at[self.job, sem], self.recv.at[self.job, sem], device)
        copy.start()
        self.sent.append(copy)
        return copy

    def add(self, index, *refs):
        total = self.part[index].astype(jnp.float32)
        for ref in refs:
            total = total + ref[...].astype(jnp.float32)
        self.part[index] = total.astype(self.part.dtype)

    def begin(self, sem, axis, block, one, two):
        p = self.place
        right, left = p.neighbour(axis, 1), p.neighbour(axis, -1)
        far, up, down = p.along(axis, 2), p.along(axis, 1), p.along(axis, -1)
        j = self.job
        self.relay = (
            self.out(sem, self.part.at[block(0, far)], one.at[j, 0], right),
            self.out(sem + 1, self.part.at[block(1, far)], one.at[j, 1], left),
        )
        self.early = (
            self.out(sem + 2, self.part.at[block(1, up)], two.at[j, 0, 1], right),
            self.out(sem + 3, self.part.at[block(0, down)], two.at[j, 1, 0], left),
        )

    def pass_on(self, sem, axis, block, one, two):
        p = self.place
        right, left = p.neighbour(axis, 1), p.neighbour(axis, -1)
        up, down = p.along(axis, 1), p.along(axis, -1)
        j = self.job
        self.relay[0].wait_recv()
        self.add(block(0, up), one.at[j, 0])
        late = self.out(sem, self.part.at[block(0, up)], two.at[j, 0, 0], right)
        self.relay[1].wait_recv()
        self.add(block(1, down), one.at[j, 1])
        self.late = (late, self.out(sem + 1, self.part.at[block(1, down)], two.at[j, 1, 1], left))

    def collect(self, axis, block, two):
        for copy in self.early + self.late:
            copy.wait_recv()
        self.add(block(slice(0, 2), self.place.at(axis)), two.at[self.job, 0], two.at[self.job, 1])

    def step(self, number):
        p = self.place
        if number == 0:
            self.begin(0, self.first, self.first_block, self.far1, self.far2)
        elif number == 1:
            self.pass_on(4, self.first, self.first_block, self.far1, self.far2)
        elif number == 2:
            self.collect(self.first, self.first_block, self.far2)
            self.begin(6, self.second, self.second_block, self.near1, self.near2)
        elif number == 3:
            self.pass_on(10, self.second, self.second_block, self.near1, self.near2)
        elif number == 4:
            self.collect(self.second, self.second_block, self.near2)
            gone = self.part.at[1 - p.zl, p.y, p.x, :, self.lanes]
            self.pair = self.out(12, gone, self.last.at[self.job], p.pair())
        else:
            self.pair.wait_recv()
            mine = self.part[p.zl, p.y, p.x, :, self.lanes].astype(jnp.float32)
            self.done(mine + self.last[self.job].astype(jnp.float32), self.lanes)

    def finish(self):
        for copy in self.sent:
            copy.wait_send()


class Swap:
    sems = 4

    def __init__(self, place, src, relay, dst, send, recv, job):
        self.place, self.src, self.relay, self.dst = place, src, relay, dst
        self.send, self.recv, self.job = send, recv, job
        self.sent = []

    def device(self, sem):
        p = self.place
        turn = p.zl if sem % 2 == 0 else 1 - p.zl
        return {"feat": p.feat(zl=1 - p.zl), "dp": lax.rem(p.dp + turn, 2)}

    def out(self, sem, src, dst):
        copy = remote(src, dst, self.send.at[self.job, sem], self.recv.at[self.job, sem], self.device(sem))
        copy.start()
        self.sent.append(copy)

    def step(self, number):
        if number == 0:
            for way in (0, 1):
                self.out(way, self.src[way], self.relay[way])
        elif number == 1:
            for way in (0, 1):
                self.sent[way].wait_recv()
                self.out(2 + way, self.relay[way], self.dst[way])
        else:
            for way in (0, 1):
                self.sent[2 + way].wait_recv()

    def finish(self):
        for copy in self.sent:
            copy.wait_send()


class Lend:
    sems = 8

    def __init__(self, place, buf, relay, rows, lanes, send, recv, job):
        p = self.place = place
        self.lanes = lanes
        half = SIDE // 2
        self.upper = p.core == 1
        self.upper_gives = jnp.logical_and(self.upper, p.dp == 0)
        self.lower_gets = jnp.logical_and(p.core == 0, p.dp == 0)
        self.over_z = p.core == 1 - p.dp
        ys = pl.ds(half * p.dp, half)
        own, far = rows.at[0, :, :, :, lanes], rows.at[1, :, :, :, lanes]
        copy = lambda sem, src, dst, device: remote(src, dst, send.at[job, sem], recv.at[job, sem], device)
        self.give_own = copy(0, buf.at[0, ys, :, :, lanes], own, p.other_core())
        self.give_far = copy(1, buf.at[2, ys, :, :, lanes], far, p.other_core())
        self.first, self.second = [], []
        for way in range(2):
            turn = p.zl if way == 0 else 1 - p.zl
            dp = lax.rem(p.dp + turn, 2)
            device = {"feat": p.feat(zl=1 - p.zl), "dp": dp}
            src = buf.at[p.dp, pl.ds(half * (1 - p.dp) + way, 1), :, :, lanes]
            self.first.append(copy(2 + way, src, relay.at[job, way], device))
            dst = rows.at[1, pl.ds(way, 1), :, :, lanes]
            self.second.append(copy(4 + way, relay.at[job, way], dst, dict(device, layer=1 - dp)))

    def step(self, number):
        if number == 0:

            @pl.when(self.upper)
            def _():
                for copy in self.first + [self.give_own]:
                    copy.start()

        elif number == 1:

            @pl.when(self.upper)
            def _():
                for way in range(2):
                    self.first[way].wait_recv()
                    self.second[way].start()

        else:

            @pl.when(self.upper_gives)
            def _():
                self.give_far.start()

    def finish(self):
        @pl.when(self.upper)
        def _():
            for copy in self.first + self.second + [self.give_own]:
                copy.wait_send()

        @pl.when(jnp.logical_not(self.upper))
        def _():
            self.give_own.wait_recv()

        @pl.when(self.upper_gives)
        def _():
            self.give_far.wait_send()

        @pl.when(self.lower_gets)
        def _():
            self.give_far.wait_recv()

        @pl.when(self.over_z)
        def _():
            for copy in self.second:
                copy.wait_recv()


def matmul(a, b, over_a=1, over_b=0):
    return lax.dot_general(a, b, (((over_a,), (over_b,)), ((), ())), preferred_element_type=jnp.float32)


CHUNKS = JOBS // 2

ORDER = (
    ("A", 6, 0), ("A", 7, 0), ("A", 4, 0), ("A", 5, 0), ("A", 2, 0), ("A", 3, 0), ("A", 0, 0), ("A", 1, 0),
    ("a", 0, 0), ("A", 6, 1), ("A", 7, 1), ("A", 4, 1), ("A", 5, 1), ("a", 1, 0), ("T", 0), ("A", 2, 1),
    ("A", 3, 1), ("a", 2, 0), ("T", 1), ("A", 0, 1), ("A", 1, 1), ("T", 2), ("a", 3, 0), ("T", 3), ("A", 6, 2),
    ("A", 7, 2), ("T", 4), ("T", 5), ("A", 4, 2), ("A", 5, 2), ("T", 6), ("T", 7), ("a", 0, 1), ("A", 2, 2),
    ("A", 3, 2), ("T", 8), ("a", 1, 1), ("T", 9), ("A", 0, 2), ("A", 1, 2), ("T", 10), ("A", 6, 3), ("A", 7, 3),
    ("T", 11), ("A", 4, 3), ("A", 5, 3), ("T", 12), ("A", 3, 3), ("T", 13), ("T", 14), ("T", 15), ("A", 2, 3),
    ("T", 16), ("A", 0, 3), ("A", 1, 3), ("T", 17), ("T", 18), ("T", 19), ("T", 20), ("T", 21), ("T", 22),
    ("T", 23), ("T", 24), ("T", 25), ("T", 26), ("T", 27), ("A", 7, 4), ("A", 6, 4), ("A", 5, 4), ("A", 4, 4),
    ("A", 3, 4), ("A", 2, 4), ("A", 1, 4), ("A", 0, 4), ("A", 7, 5), ("A", 6, 5), ("L", 3), ("F", 3), ("A", 5, 5),
    ("A", 4, 5), ("L", 2), ("a", 2, 1), ("a", 3, 1), ("A", 3, 5), ("A", 2, 5), ("L", 1), ("F", 2), ("D", 3, 0),
    ("D", 3, 1), ("R", 6, 0), ("R", 7, 0), ("S", 3, 1), ("D", 2, 0), ("D", 2, 1), ("R", 4, 0), ("R", 5, 0),
    ("R", 6, 1), ("R", 7, 1), ("S", 3, 2), ("S", 2, 1), ("F", 1), ("A", 1, 5), ("A", 0, 5), ("L", 0), ("R", 4, 1),
    ("R", 5, 1), ("S", 2, 2), ("D", 1, 0), ("D", 1, 1), ("R", 2, 0), ("R", 3, 0), ("S", 1, 1), ("R", 6, 2),
    ("R", 7, 2), ("F", 0), ("R", 4, 2), ("R", 5, 2), ("S", 1, 2), ("R", 2, 1), ("R", 3, 1), ("D", 0, 0),
    ("R", 7, 3), ("R", 6, 3), ("R", 5, 3), ("R", 4, 3), ("D", 0, 1), ("R", 0, 0), ("R", 1, 0), ("S", 0, 1),
    ("R", 2, 2), ("R", 7, 4), ("R", 6, 4), ("R", 5, 4), ("R", 4, 4), ("R", 3, 2), ("R", 0, 1), ("R", 1, 1),
    ("R", 7, 5), ("G", 7, 0), ("R", 6, 5), ("G", 6, 0), ("R", 5, 5), ("G", 5, 0), ("R", 4, 5), ("G", 4, 0),
    ("S", 0, 2), ("g", 2, 0), ("R", 3, 3), ("g", 3, 0), ("R", 2, 3), ("a", 1, 2), ("G", 7, 1), ("a", 0, 2),
    ("G", 6, 1), ("G", 5, 1), ("G", 4, 1), ("R", 0, 2), ("R", 3, 4), ("R", 2, 4), ("R", 1, 2), ("a", 2, 2),
    ("G", 7, 2), ("a", 3, 2), ("G", 6, 2), ("a", 0, 3), ("R", 3, 5), ("G", 3, 0), ("R", 2, 5), ("G", 5, 2),
    ("G", 2, 0), ("G", 4, 2), ("g", 1, 0), ("a", 1, 3), ("R", 1, 3), ("R", 0, 3), ("G", 7, 3), ("G", 3, 1),
    ("G", 2, 1), ("G", 6, 3), ("G", 4, 3), ("G", 5, 3), ("R", 1, 4), ("R", 0, 4), ("G", 3, 2), ("R", 1, 5),
    ("G", 1, 0), ("R", 0, 5), ("G", 0, 0), ("g", 0, 0), ("G", 1, 1), ("G", 0, 1), ("G", 7, 4), ("G", 6, 4),
    ("G", 2, 2), ("G", 4, 4), ("G", 5, 4), ("G", 3, 3), ("G", 0, 2), ("G", 1, 2), ("G", 7, 5), ("G", 6, 5),
    ("M", 3), ("g", 3, 1), ("G", 2, 3), ("B", 3, 0), ("G", 4, 5), ("G", 5, 5), ("M", 2), ("G", 1, 3), ("W", 3),
    ("B", 2, 0), ("B", 3, 1), ("W", 2), ("G", 3, 4), ("a", 2, 3), ("B", 2, 1), ("G", 2, 4), ("G", 0, 3),
    ("P", 3, 1), ("g", 2, 1), ("G", 1, 4), ("G", 3, 5), ("a", 3, 3), ("G", 2, 5), ("M", 1), ("P", 2, 1),
    ("B", 1, 0), ("G", 1, 5), ("g", 1, 1), ("a", 0, 4), ("P", 3, 2), ("a", 1, 4), ("G", 0, 4), ("B", 1, 1),
    ("W", 1), ("g", 0, 1), ("g", 3, 2), ("g", 2, 2), ("P", 2, 2), ("a", 0, 5), ("a", 2, 4), ("a", 3, 4),
    ("a", 1, 5), ("G", 0, 5), ("M", 0), ("P", 1, 1), ("g", 1, 2), ("g", 0, 2), ("g", 2, 3), ("g", 3, 3),
    ("B", 0, 0), ("a", 2, 5), ("a", 3, 5), ("W", 0), ("B", 0, 1), ("g", 1, 3), ("g", 0, 3), ("P", 1, 2),
    ("g", 2, 4), ("g", 3, 4), ("P", 0, 1), ("g", 0, 4), ("g", 1, 4), ("g", 2, 5), ("g", 3, 5), ("P", 0, 2),
    ("g", 0, 5), ("g", 1, 5),
)


def band_kernel(
    scale, acts_in, target_ref, bias_ref, enc_bias_ref, enc_in, dec_in, cross_in,
    resid_ref, acts_buf, grad_buf, feats_out, lower_out, far_out, far_lower_ref, pre_ref, far_pre_ref, rows_buf,
    relay, pre_relay, rows_relay, acts_relay,
    enc_n, dec_n, enc_t, dec_t, cross_t, cross_ref, feats_ref, lower_ref, far_ref, bias_t, enc_bias_t, positive_ref, down_ref, up_ref,
    chunk, part, shard, far1, far2, near1, near2, last,
    send_a, recv_a, send_r, recv_r, send_g, recv_g, send_s, recv_s, send_p, recv_p, send_l, recv_l,
    send_xa, recv_xa, send_xg, recv_xg, send_z, recv_z,
    local_a, local_g, load_sem, chunk_sem, grad_sem, out_sem, core_send, core_recv,
):
    tokens = acts_in.shape[1]
    wide = tokens // CHUNKS
    lane = wide // 2
    rows = acts_in.shape[0]
    n_feat = feats_ref.shape[0]
    half = cross_ref.shape[2]
    width = 2 * half
    place = Place()
    first_core = place.core == 0

    loads = [
        pltpu.make_async_copy(enc_in, enc_n, load_sem.at[0]),
        pltpu.make_async_copy(dec_in, dec_n, load_sem.at[1]),
        pltpu.make_async_copy(cross_in, cross_ref.at[place.core], load_sem.at[2]),
    ]
    for load in loads:
        load.start()
    place.greet()

    def swap_cross():
        at = 3 * CHUNKS
        copy = remote(cross_in, cross_ref.at[place.core], core_send.at[at], core_recv.at[at], place.other_core())
        copy.start()
        return copy

    def finish_residual(total, lanes):
        resid = total + bias_t[:, 0:1] - target_ref[:, lanes].astype(jnp.float32)
        resid_ref[:, lanes] = resid
        shard[:, lanes] = (resid * scale).astype(shard.dtype)

    room = (far1, far2, near1, near2, last)
    gathers, reduces, grads, swaps, lent, far_lent, pre_swaps, lends, downs = [], [], [], [], [], [], [], [], []
    act_extras, grad_extras, act_swaps = [], [], []
    for job in range(JOBS):
        c, flip = job // 2, job % 2
        lanes = pl.ds(job * lane, lane)
        gathers.append(
            Gather(place, acts_buf, acts_in.at[:, lanes], lanes, flip, send_a, recv_a, local_a, job)
        )
        grads.append(Gather(place, grad_buf, shard.at[:, lanes], lanes, flip, send_g, recv_g, local_g, job))
        inner = pl.ds(flip * lane, lane)
        done = functools.partial(lambda whole, total, _: finish_residual(total, whole), lanes)
        reduces.append(Reduce(place, part.at[c], inner, flip, room, send_r, recv_r, job, done))
    for c in range(CHUNKS):
        lanes = pl.ds(c * wide, wide)
        ways = [pl.ds(way * (n_feat // 2), n_feat // 2) for way in (0, 1)]

        def dp_swap(here, between, there, send, recv):
            return Swap(
                place, [here.at[w, lanes] for w in ways], [between.at[c, way] for way in (0, 1)],
                [there.at[w, lanes] for w in ways], send, recv, c,
            )

        def to_core(kind, here, there):
            at = kind * CHUNKS + c
            return remote(
                here.at[:, lanes], there.at[:, lanes], core_send.at[at], core_recv.at[at], place.other_core()
            )

        swaps.append(dp_swap(feats_ref, relay, far_ref, send_s, recv_s))
        pre_swaps.append(dp_swap(pre_ref, pre_relay, far_pre_ref, send_p, recv_p))
        lent.append(to_core(0, feats_ref, lower_ref))
        far_lent.append(to_core(1, far_ref, far_lower_ref))
        downs.append(to_core(2, down_ref, up_ref))
        act_extras.append(
            Extra(place, acts_buf, acts_in.at[:, lanes], lanes, c % 2, send_xa, recv_xa, None, c)
        )
        grad_extras.append(Extra(place, grad_buf, shard.at[:, lanes], lanes, c % 2, send_xg, recv_xg, None, c))
        y_halves = [pl.ds(way * (SIDE // 2), SIDE // 2) for way in (0, 1)]
        act_swaps.append(
            Swap(
                place, [acts_buf.at[1 - place.dp, ys, :, :, lanes] for ys in y_halves],
                [acts_relay.at[c, way] for way in (0, 1)], [acts_buf.at[2, ys, :, :, lanes] for ys in y_halves],
                send_z, recv_z, c,
            )
        )
        lends.append(Lend(place, grad_buf, rows_relay, rows_buf, lanes, send_l, recv_l, c))

    def load_chunk(c):
        return pltpu.make_async_copy(
            acts_buf.at[pl.ds(0, 2), :, :, :, pl.ds(c * wide, wide)], chunk.at[c % 2], chunk_sem.at[c]
        )

    def encode(c):
        load_chunk(c).wait()
        lanes = pl.ds(c * wide, wide)
        pre_act = matmul(enc_t[...], chunk[c % 2].reshape(width, wide)) + enc_bias_t[:, 0:1]
        positive = jnp.maximum(pre_act, 0.0)
        positive_ref[:, lanes] = positive
        feats_ref[:, lanes] = (positive * positive).astype(feats_ref.dtype)

        @pl.when(first_core)
        def _():
            lent[c].start()
            lower_ref[:, lanes] = feats_ref[:, lanes]

        swaps[c].step(0)

    outs = [
        pltpu.make_async_copy(here, there, out_sem.at[i])
        for i, (here, there) in enumerate([(feats_ref, feats_out), (lower_ref, lower_out), (far_ref, far_out)])
    ]
    lent_far = []

    def lend_far(c):
        swaps[c].step(2)
        lent_far.append(c)
        if len(lent_far) == CHUNKS:
            for copy in outs:
                copy.start()
        lanes = pl.ds(c * wide, wide)

        @pl.when(first_core)
        def _():
            far_lent[c].start()
            far_lower_ref[:, lanes] = far_ref[:, lanes]

    def decode(c, side):
        lanes = pl.ds(c * wide, wide)
        block = SIDE * rows

        def store(i, total):
            part[c, lax.div(i, SIDE), lax.rem(i, SIDE)] = total.astype(part.dtype).reshape(SIDE, rows, wide)

        def at(i):
            return pl.ds(pl.multiple_of(i * block, 16), block)

        @pl.when(first_core)
        def _():
            @pl.loop(side * SIDE, side * SIDE + SIDE)
            def _(i):
                store(i, matmul(dec_t[at(i), :], feats_ref[:, lanes]))

        @pl.when(jnp.logical_not(first_core))
        def _():
            if side == 0:
                lent[c].wait_recv()

            @pl.loop(side * SIDE, side * SIDE + SIDE)
            def _(i):
                total = matmul(dec_t[at(i), :], feats_ref[:, lanes]) + matmul(cross_t[at(i), :], lower_ref[:, lanes])
                store(i, total)

    def load_grads(c):
        return pltpu.make_async_copy(
            grad_buf.at[pl.ds(0, 2), :, :, :, pl.ds(c * wide, wide)], chunk.at[c % 2], grad_sem.at[c]
        )

    def finish_grads(c):
        load_grads(c).start()
        lends[c].step(0)

    def extra_grads(c, number):
        grad_extras[c].step(number)
        if number == Gather.steps - 1:
            lends[c].step(2)

    def backward(c, part):
        lanes = pl.ds(c * wide, wide)
        here = chunk.at[c % 2]
        if part == 0:
            load_grads(c).wait()
            send_down(c, lanes, here)
        else:
            make_pre(c, lanes, here)

    def send_down(c, lanes, here):
        @pl.when(jnp.logical_not(first_core))
        def _():
            down = matmul(cross_ref[0], here[0].reshape(half, wide)) + matmul(cross_ref[1], here[1].reshape(half, wide))
            down_ref[:, lanes] = down.astype(down_ref.dtype)
            downs[c].start()

    def make_pre(c, lanes, here):
        grad_feats = matmul(dec_n[...], here[...].reshape(width, wide))

        @pl.when(first_core)
        def _():
            downs[c].wait_recv()
            total = grad_feats + up_ref[:, lanes].astype(jnp.float32)
            pre_ref[:, lanes] = (total * 2.0 * positive_ref[:, lanes]).astype(pre_ref.dtype)

        @pl.when(jnp.logical_not(first_core))
        def _():
            pre_ref[:, lanes] = (grad_feats * 2.0 * positive_ref[:, lanes]).astype(pre_ref.dtype)

        pre_swaps[c].step(0)

    cross_swap = []

    def turn_enc(i):
        if i == 0:
            bias_t[...] = jnp.broadcast_to(bias_ref[...], (128, rows)).T
            enc_bias_t[...] = jnp.broadcast_to(enc_bias_ref[...], (128, n_feat)).T
            loads[0].wait()
        block = pl.ds(i * n_feat, n_feat)
        enc_t[:, block] = enc_n[block, :].T

    def turn_dec(i):
        if i == 0:
            loads[1].wait()
        block = pl.ds(i * n_feat, n_feat)
        dec_t[block, :] = dec_n[:, block].T

    def turn_cross(i):
        if i == 0:
            loads[2].wait()
            cross_swap[0].wait_recv()
        z, at = divmod(i * 256, half)
        cross_t[pl.ds(i * 256, 256), :] = cross_ref[z, :, pl.ds(at, 256)].T

    background = [functools.partial(turn_enc, i) for i in range(width // n_feat)]
    background += [functools.partial(turn_dec, i) for i in range(width // n_feat)]
    background += [functools.partial(turn_cross, i) for i in range(width // 256)]

    cross_swap.append(swap_cross())
    act_jobs = {
        "A": lambda i, n: gathers[i].step(n),
        "a": lambda i, n: act_extras[i].step(n),
        "Z": lambda i, n: act_swaps[i].step(n),
        "T": lambda i: background[i](),
        "L": lambda i: load_chunk(i).start(),
        "F": encode,
        "D": decode,
        "R": lambda i, n: reduces[i].step(n),
        "G": lambda i, n: grads[i].step(n),
        "g": extra_grads,
        "M": finish_grads,
        "B": backward,
        "S": lambda i, n: swaps[i].step(1) if n == 1 else lend_far(i),
        "P": lambda i, n: pre_swaps[i].step(n),
        "W": lambda i: lends[i].step(1),
    }
    for name, *numbers in ORDER:
        act_jobs[name](*numbers)
    used = {(name, numbers[0]) for name, *numbers in ORDER}
    act_extras = [job for i, job in enumerate(act_extras) if ("a", i) in used]
    act_swaps = [job for i, job in enumerate(act_swaps) if ("Z", i) in used]
    everything = gathers + act_extras + act_swaps + reduces + grads + grad_extras + swaps + pre_swaps + lends
    for job in everything:
        job.finish()
    cross_swap[0].wait_send()
    for copy in outs:
        copy.wait()

    @pl.when(first_core)
    def _():
        for copy in lent + far_lent:
            copy.wait_send()

    @pl.when(jnp.logical_not(first_core))
    def _():
        for copy in far_lent:
            copy.wait_recv()
        for copy in downs:
            copy.wait_send()


def band(acts, targets, bias, enc_bias, enc, dec_own, dec_cross, scale):
    rows, tokens = targets.shape
    width, n_feat = enc.shape
    lane = tokens // JOBS
    wide = tokens // CHUNKS
    kind = acts.dtype
    whole = pl.BlockSpec(memory_space=pltpu.VMEM)
    away = pl.BlockSpec(memory_space=pl.ANY)
    gathered = jax.ShapeDtypeStruct((3, SIDE, SIDE, rows, tokens), kind)
    feats = jax.ShapeDtypeStruct((n_feat, tokens), kind)
    dma = pltpu.SemaphoreType.DMA
    return pl.pallas_call(
        functools.partial(band_kernel, scale),
        out_shape=(
            jax.ShapeDtypeStruct((rows, tokens), jnp.float32),
            gathered,
            gathered,
            feats, feats, feats, feats, feats, feats,
            jax.ShapeDtypeStruct((2, SIDE // 2, SIDE, rows, tokens), kind),
            jax.ShapeDtypeStruct((CHUNKS, 2, n_feat // 2, wide), kind),
            jax.ShapeDtypeStruct((CHUNKS, 2, n_feat // 2, wide), kind),
            jax.ShapeDtypeStruct((CHUNKS, 2, 1, SIDE, rows, wide), kind),
            jax.ShapeDtypeStruct((CHUNKS, 2, SIDE // 2, SIDE, rows, wide), kind),
        ),
        in_specs=[whole] * 4 + [away] * 3,
        out_specs=(whole, away, away) + (away,) * 3 + (whole,) * 3 + (away,) * 5,
        scratch_shapes=[
            pltpu.VMEM((width, n_feat), kind),
            pltpu.VMEM((n_feat, width), kind),
            pltpu.VMEM((n_feat, width), kind),
            pltpu.VMEM((width, n_feat), kind),
            pltpu.VMEM((width, n_feat), kind),
            pltpu.VMEM((2,) + dec_cross.shape, kind),
            pltpu.VMEM((n_feat, tokens), kind),
            pltpu.VMEM((n_feat, tokens), kind),
            pltpu.VMEM((n_feat, tokens), kind),
            pltpu.VMEM((rows, 128), jnp.float32),
            pltpu.VMEM((n_feat, 128), jnp.float32),
            pltpu.VMEM((n_feat, tokens), jnp.float32),
            pltpu.VMEM((n_feat, tokens), kind),
            pltpu.VMEM((n_feat, tokens), kind),
            pltpu.VMEM((2, 2, SIDE, SIDE, rows, wide), kind),
            pltpu.VMEM((CHUNKS, 2, SIDE, SIDE, rows, wide), kind),
            pltpu.VMEM((rows, tokens), kind),
            pltpu.VMEM((JOBS, 2, SIDE, rows, lane), kind),
            pltpu.VMEM((JOBS, 2, 2, SIDE, rows, lane), kind),
            pltpu.VMEM((JOBS, 2, rows, lane), kind),
            pltpu.VMEM((JOBS, 2, 2, rows, lane), kind),
            pltpu.VMEM((JOBS, rows, lane), kind),
            dma((JOBS, Gather.sems)),
            dma((JOBS, Gather.sems)),
            dma((JOBS, Reduce.sems)),
            dma((JOBS, Reduce.sems)),
            dma((JOBS, Gather.sems)),
            dma((JOBS, Gather.sems)),
            dma((CHUNKS, Swap.sems)),
            dma((CHUNKS, Swap.sems)),
            dma((CHUNKS, Swap.sems)),
            dma((CHUNKS, Swap.sems)),
            dma((CHUNKS, Lend.sems)),
            dma((CHUNKS, Lend.sems)),
            dma((CHUNKS, Gather.sems)),
            dma((CHUNKS, Gather.sems)),
            dma((CHUNKS, Gather.sems)),
            dma((CHUNKS, Gather.sems)),
            dma((CHUNKS, Swap.sems)),
            dma((CHUNKS, Swap.sems)),
            dma((JOBS,)),
            dma((JOBS,)),
            dma((3,)),
            dma((CHUNKS,)),
            dma((CHUNKS,)),
            dma((3,)),
            dma((3 * CHUNKS + 1,)),
            dma((3 * CHUNKS + 1,)),
        ],
        compiler_params=pltpu.CompilerParams(
            collective_id=1, has_side_effects=True, vmem_limit_bytes=60 * 1024 * 1024
        ),
        name="band",
    )(acts, targets, bias, enc_bias, enc, dec_own, dec_cross)


def weights_kernel(
    acts_in, grads_in, rows_in, feats_in, far_in, first_in, far_first_in, pre_in, far_pre_in,
    enc_out, own_out, cross_out,
    acts, grads, rows, feats, first, pre, enc_g, own_g, cross_g, load_sem, store_sem,
):
    dp = lax.axis_index("dp")
    half = SIDE // 2
    n_feat, width = own_g.shape
    block = width // 2
    started = []

    def load(src, dst):
        copy = pltpu.make_async_copy(src, dst, load_sem.at[len(started)])
        copy.start()
        started.append(copy)
        return copy

    ys = [pl.ds(half * part, half) for part in (0, 1)]
    first_loads = [load(feats_in, feats.at[0]), load(far_in, feats.at[1])]
    grad_loads = [[load(grads_in.at[slot, y], grads.at[i, y]) for i, slot in ((0, dp), (1, 2))] for y in ys]
    pre_loads = [load(pre_in, pre.at[0]), load(far_pre_in, pre.at[1])]
    act_loads = [[load(acts_in.at[slot, y], acts.at[i, y]) for i, slot in ((0, dp), (1, 2))] for y in ys]
    cross_loads = [load(first_in, first.at[0]), load(far_first_in, first.at[1])]
    upper = lax.axis_index("layer") == 1
    mine = pl.ds(half * dp, half)

    def load_rows(i, here, slot):
        at = len(started)

        @pl.when(here)
        def _():
            pltpu.make_async_copy(grads_in.at[slot, mine], rows.at[i], load_sem.at[at]).start()

        @pl.when(jnp.logical_not(here))
        def _():
            pltpu.make_async_copy(rows_in.at[i], rows.at[i], load_sem.at[at]).start()

        started.append(pltpu.make_async_copy(rows_in.at[i], rows.at[i], load_sem.at[at]))
        return started[-1]

    cross_loads += [load_rows(0, upper, 1), load_rows(1, jnp.logical_and(upper, dp == 1), 2)]
    stores = []

    def store(src, dst):
        copy = pltpu.make_async_copy(src, dst, store_sem.at[len(stores)])
        copy.start()
        stores.append(copy)

    def both(a, b):
        return matmul(a[0], b[0], 1, 1) + matmul(a[1], b[1], 1, 1)

    def by_feats(left, right, out, columns):
        out[:, columns] = both((left[0], left[1]), right())

    for copy in first_loads:
        copy.wait()
    for part in (0, 1):
        for copy in grad_loads[part]:
            copy.wait()
        columns = pl.ds(part * block, block)
        by_feats(feats, lambda: [grads[i, ys[part]].reshape(block, -1) for i in (0, 1)], own_g, columns)
        store(own_g.at[:, columns], own_out.at[:, columns])
    for copy in pre_loads:
        copy.wait()
    for part in (0, 1):
        for copy in act_loads[part]:
            copy.wait()
        for y in range(half * part, half * part + half):
            at = pl.ds(y * (width // SIDE), width // SIDE)
            enc_g[at, :] = both([acts[i, y].reshape(width // SIDE, -1) for i in (0, 1)], [pre[0], pre[1]])
            store(enc_g.at[at, :], enc_out.at[at, :])
    for copy in cross_loads:
        copy.wait()
    by_feats(first, lambda: [rows[i].reshape(block, -1) for i in (0, 1)], cross_g, pl.ds(0, block))
    store(cross_g, cross_out)
    for copy in stores:
        copy.wait()


def weights(acts, grads, lent, feats, far, first, far_first, pre, far_pre):
    rows, tokens = acts.shape[3:]
    n_feat = feats.shape[0]
    half = SIDE * SIDE * rows
    kind = acts.dtype
    f32 = jnp.float32
    away = pl.BlockSpec(memory_space=pl.ANY)
    shapes = [(half, n_feat), (n_feat, half), (n_feat, half // 2)]
    return pl.pallas_call(
        weights_kernel,
        out_shape=[jax.ShapeDtypeStruct(s, f32) for s in shapes],
        in_specs=[away] * 9,
        out_specs=[away] * 3,
        scratch_shapes=[
            pltpu.VMEM((2, SIDE, SIDE, rows, tokens), kind),
            pltpu.VMEM((2, SIDE, SIDE, rows, tokens), kind),
            pltpu.VMEM(lent.shape, kind),
            pltpu.VMEM((2, n_feat, tokens), kind),
            pltpu.VMEM((2, n_feat, tokens), kind),
            pltpu.VMEM((2, n_feat, tokens), kind),
        ]
        + [pltpu.VMEM(s, f32) for s in shapes]
        + [pltpu.SemaphoreType.DMA((16,)), pltpu.SemaphoreType.DMA((8,))],
        compiler_params=pltpu.CompilerParams(vmem_limit_bytes=60 * 1024 * 1024),
        name="weights",
    )(acts, grads, lent, feats, far, first, far_first, pre, far_pre)


def local(acts, targets, enc, enc_bias, dec_own, dec_cross, dec_bias):
    tokens, rows = acts.shape[1:]
    scale = float(tokens * lax.axis_size("dp")) ** (-0.5)
    bias = dec_bias.astype(jnp.float32)
    residual, gathered, grads, feats, first, far, far_first, pre, far_pre, lent = band(
        acts[0].T, targets[0].T, bias, enc_bias, enc[0], dec_own[0], dec_cross, scale
    )[:10]
    grad_enc, grad_own, grad_cross = weights(gathered, grads, lent, feats, far, first, far_first, pre, far_pre)
    return (residual.T[None], grad_enc[None], grad_own[None], grad_cross)


def solution(mesh):
    in_specs = (
        P("layer", "dp", "feat"),
        P("layer", "dp", "feat"),
        P("layer", None, "feat"),
        P("layer", "feat"),
        P("layer", "feat", None),
        P("feat", "layer"),
        P("layer", "feat"),
    )
    out_specs = (
        P("layer", "dp", "feat"),
        P("layer", "dp", "feat"),
        P("layer", "feat", "dp"),
        P("feat", ("layer", "dp")),
    )
    return jax.shard_map(local, mesh=mesh, in_specs=in_specs, out_specs=out_specs, check_vma=False)
```

profile of v0, /device:TPU:1, one launch (start us, length us, event | category | flops | bytes accessed | tf_op | source)
XLA Modules:
  0.0 197.8 jit_solution(780669369277308172)
XLA Ops:
  0.6 1.2 convert_element_type.3.bias_ref
  1.8 179.7 %band.1 = (f32[112,1024]{1,0:T(8,128)}, bf16[3,4,4,112,1024]{4,3,2,1,0:T(8,128)(2,1)}, bf16[3,4,4,112,1024]{4,3,2,1,0:T(8,128)(2,1)}, bf16[512,1024]{1,0:T(8,128...) custom-call(bf16[112,1024]{1,0:T(8,128)(2,1)} %bitcast.16, ...), custom_call_target="tpu_custom_call" | custom-call | tf_op jit(solution)/shard_map/band/pallas_call | solution.py:690
  181.5 0.0 copy-start
  181.5 15.5 %weights.1 = (f32[1792,512]{1,0:T(8,128)}, f32[512,1792]{1,0:T(8,128)}, f32[512,896]{1,0:T(8,128)}) custom-call(bf16[3,4,4,112,1024]{4,3,2,1,0:T(8,128)(2,1)} %get-tuple-element.18.acts_in, bf16[3,4,4,112,1024]{4,3,2,1,0:T(8,128)(2,1)} %get-tuple-element.19.grads_in, bf16[2,2,4,112,1024]{4,3,2,1,0:T(8,128)(2,1)} %get-tuple-element.20.rows_in, ...), custom_call_target="tpu_custom_call" | custom-call | tf_op jit(solution)/shard_map/weights/pallas_call | solution.py:849
  197.0 0.0 copy-done
  197.0 0.8 copy.12
Async XLA Ops:
  181.5 15.5 %copy-start = (f32[112,1024]{1,0:T(8,128)S(1)}, f32[112,1024]{1,0:T(8,128)}, u32[]{:S(2)}) copy-start(f32[112,1024]{1,0:T(8,128)} %get-tuple-element.17) | copy-start | bytes 1376260
where the time goes:
time: 198 us
  Pallas kernels  195 us (98%)
    pallas_call x1, Pallas kernels, band(): pl.pallas_call(functools.partial(band_kernel, scale), out_shape=(jax.Shap...  180 us
    pallas_call x1, Pallas kernels, weights(): pl.pallas_call(weights_kernel, out_shape=[jax.ShapeDtypeStruct(s, f32) fo...  15.5 us

commit v1 on v0

--- a/solution.py
+++ b/solution.py
@@ -110,14 +110,16 @@
     def begin(self):
         p = self.place
         here = self.buf.at[p.zl, p.y, p.x, :, self.lanes]
-        self.kept = pltpu.make_async_copy(self.own, here, self.local.at[self.job])
-        self.kept.start()
+        if self.local is not None:
+            self.kept = [pltpu.make_async_copy(self.own, here, self.local.at[self.job])]
+            self.kept[0].start()
         self.waits = [self.copy(0, self.own, here, p.pair())]
         self.waits[0].start()
         self.sent += self.waits
 
     def settle(self):
-        self.kept.wait()
+        while self.kept:
+            self.kept.pop().wait()
 
     def step(self, number):
         if number == 0:
@@ -455,7 +457,7 @@
         c, flip = job // 2, job % 2
         lanes = pl.ds(job * lane, lane)
         gathers.append(
-            Gather(place, acts_buf, acts_in.at[:, lanes], lanes, flip, send_a, recv_a, local_a, job)
+            Gather(place, acts_buf, acts_in.at[:, lanes], lanes, flip, send_a, recv_a, None, job)
         )
         grads.append(Gather(place, grad_buf, shard.at[:, lanes], lanes, flip, send_g, recv_g, local_g, job))
         inner = pl.ds(flip * lane, lane)
@@ -634,6 +636,10 @@
     background += [functools.partial(turn_cross, i) for i in range(width // 256)]
 
     cross_swap.append(swap_cross())
+    kept = [pltpu.make_async_copy(acts_in, acts_buf.at[place.zl, place.y, place.x], local_a.at[0])]
+    kept[0].start()
+    for job in gathers:
+        job.kept = kept
     act_jobs = {
         "A": lambda i, n: gathers[i].step(n),
         "a": lambda i, n: act_extras[i].step(n),

time: 198 us -> 198 us (level)
  no operation moved by 1% of the time
where the time goes in v1:
time: 198 us
  Pallas kernels  195 us (98%)
    pallas_call x1, Pallas kernels, band(): pl.pallas_call(functools.partial(band_kernel, scale), out_shape=(jax.Shap...  180 us
    pallas_call x1, Pallas kernels, weights(): pl.pallas_call(weights_kernel, out_shape=[jax.ShapeDtypeStruct(s, f32) fo...  15.5 us

profile of v1, /device:TPU:1, one launch (start us, length us, event | category | flops | bytes accessed | tf_op | source)
XLA Modules:
  0.0 197.8 jit_solution(11595113051836968719)
XLA Ops:
  0.6 1.2 convert_element_type.3.bias_ref
  1.8 179.7 %band.1 = (f32[112,1024]{1,0:T(8,128)}, bf16[3,4,4,112,1024]{4,3,2,1,0:T(8,128)(2,1)}, bf16[3,4,4,112,1024]{4,3,2,1,0:T(8,128)(2,1)}, bf16[512,1024]{1,0:T(8,128...) custom-call(bf16[112,1024]{1,0:T(8,128)(2,1)} %bitcast.16, ...), custom_call_target="tpu_custom_call" | custom-call | tf_op jit(solution)/shard_map/band/pallas_call | solution.py:696
  181.5 0.0 copy-start
  181.5 15.5 %weights.1 = (f32[1792,512]{1,0:T(8,128)}, f32[512,1792]{1,0:T(8,128)}, f32[512,896]{1,0:T(8,128)}) custom-call(bf16[3,4,4,112,1024]{4,3,2,1,0:T(8,128)(2,1)} %get-tuple-element.18.acts_in, bf16[3,4,4,112,1024]{4,3,2,1,0:T(8,128)(2,1)} %get-tuple-element.19.grads_in, bf16[2,2,4,112,1024]{4,3,2,1,0:T(8,128)(2,1)} %get-tuple-element.20.rows_in, ...), custom_call_target="tpu_custom_call" | custom-call | tf_op jit(solution)/shard_map/weights/pallas_call | solution.py:855
  197.0 0.0 copy-done
  197.0 0.8 copy.12
Async XLA Ops:
  181.5 15.5 %copy-start = (f32[112,1024]{1,0:T(8,128)S(1)}, f32[112,1024]{1,0:T(8,128)}, u32[]{:S(2)}) copy-start(f32[112,1024]{1,0:T(8,128)} %get-tuple-element.17) | copy-start | bytes 1376260
